TPU v7x, 32 devices: a whole 2x2x4 slice. The times are simulated.
32 devices in a mesh: dp: 4 (over y, core), mp: 8 (over z, x).
Axes of the slice: x: 2, y: 2, z: 4, core: 2. Of those that a mesh axis runs over, the one named last changes fastest.
Arguments:
- tokens: bfloat16 [4096, 2048], P(('dp', 'mp')), may hold values from -6 to 6
- norm_gain: float32 [2048], replicated, may hold values from 0.1 to 1.9
- router: bfloat16 [2048, 8], replicated, may hold values from -0.125 to 0.125
- routes: int32 [4096, 2], P(('dp', 'mp')), may hold values from 0 to 7, all different within a row; in each aligned block of 128 rows (0 to 127, 128 to 255, ...) at most 40 rows name the same one
- prompt_lengths: int32 [8], replicated, may hold values from 256 to 512, as said below
- wq_train: float32 [8, 2048, 2048], P(None, ('dp', 'mp'))
- wo_train: float32 [8, 2048, 2048], P(None, ('dp', 'mp')), may hold values from -0.25 to 0.25
- wkv_train: float32 [2048, 4096], P(('dp', 'mp'))
- page_table: int32 [4, 8, 8], P('dp', 'mp'), may hold values from 0 to 127, as said below
Outputs:
- attn_out: bfloat16 [4096, 2048], P(('dp', 'mp'))
- kv_pool: bfloat16 [512, 16, 4096], P(('dp', 'mp'))
Inputs may be any that keep to these rules, and one draw needn't show every extreme that they name: `routes`: each of the two entries of a row names a different expert; in the rows of one device (aligned blocks of 128 rows) no expert is named by more than 40 rows, a bound that some block reaches. `prompt_lengths`: every prompt uses at least 256 slots; some prompt uses all 512 and another exactly 256. `page_table`: entry [g, w, q] equals owner * 16 + w * 2 + c with c < 2; the pairs (owner, c) of one writer w in one group are distinct, so at most 2 pages of one writer go to one owner. In every group one owner receives 2 pages from every writer. Pool pages that no entry names stay zero.
All inputs are finite; a program needn't handle non-finite values.
Results may differ from a plain program's by a relative error of at most 0.012.
The roundings to bfloat16 on the way count: a program that leaves them out, or rounds other values in their place, can miss the bound.
Values may be sent and summed in bfloat16 or wider, within the bound.
A program may use at most 192 MiB of HBM per device.

v0:
```python
import jax
import jax.numpy as jnp
from jax import lax
from jax.sharding import PartitionSpec as P

HD = 128
PAGE = 16
PCAP = 2


def rotate(vectors, positions):
    half_dim = vectors.shape[-1] // 2
    frequency = 10000.0 ** (-(jnp.arange(half_dim, dtype=jnp.float32) * 2.0 / vectors.shape[-1]))
    angles = positions.astype(jnp.float32)[:, None] * frequency[None, :]
    cosine = jnp.cos(angles)[:, None, :]
    sine = jnp.sin(angles)[:, None, :]
    leading = vectors[..., :half_dim]
    trailing = vectors[..., half_dim:]
    return jnp.concatenate(
        [leading * cosine - trailing * sine, trailing * cosine + leading * sine], axis=-1
    )


def on_device(
    tokens, norm_gain, router, routes, prompt_lengths, wq_train, wo_train, wkv_train, page_table
):
    mp_count = lax.axis_size("mp")
    experts = wq_train.shape[0]
    blocks = mp_count // experts
    width = wq_train.shape[2]
    block_width = width // blocks
    head_dim = HD
    block_heads = block_width // head_dim
    tok_rows = tokens.shape[0]
    model_width = tokens.shape[1]
    capacity = tok_rows // 4 + tok_rows // 16
    prompt_len = tok_rows * mp_count // 2
    writer_pages = tok_rows * blocks // PAGE
    slot_count = mp_count * PCAP
    device = lax.axis_index("mp")
    expert = device // blocks
    prompt_group = lax.axis_index("dp")
    shard_rows = wq_train.shape[1]
    query_part = wq_train.reshape(experts, shard_rows, blocks, block_width).transpose(0, 2, 1, 3)
    query_part = query_part.reshape(mp_count, shard_rows, block_width).astype(jnp.bfloat16)
    output_part = wo_train.reshape(experts, shard_rows, blocks, block_width).transpose(0, 2, 1, 3)
    output_part = output_part.reshape(mp_count, shard_rows, block_width).astype(jnp.bfloat16)
    pair_part = wkv_train.reshape(shard_rows, 2, blocks, block_width).transpose(2, 0, 1, 3)
    pair_part = pair_part.reshape(blocks, shard_rows, 2 * block_width)
    pair_part = jnp.broadcast_to(pair_part[None], (experts, blocks, shard_rows, 2 * block_width))
    pair_part = pair_part.reshape(mp_count, shard_rows, 2 * block_width).astype(jnp.bfloat16)
    exchanged = (
        lax.all_to_all(query_part, "mp", split_axis=0, concat_axis=1, tiled=True),
        lax.all_to_all(output_part, "mp", split_axis=0, concat_axis=1, tiled=True),
        lax.all_to_all(pair_part, "mp", split_axis=0, concat_axis=1, tiled=True),
    )
    query_w, output_w, pair_w = (
        lax.all_gather(exchanged[0], "dp", axis=1, tiled=True),
        lax.all_gather(exchanged[1], "dp", axis=1, tiled=True),
        lax.all_gather(exchanged[2], "dp", axis=1, tiled=True),
    )
    query_w = query_w[0]
    output_w = output_w[0]
    pair_w = pair_w[0]
    wide_tokens = tokens.astype(jnp.float32)
    normed = (
        wide_tokens
        * lax.rsqrt(jnp.mean(wide_tokens * wide_tokens, axis=-1, keepdims=True) + 1e-06)
        * norm_gain
    ).astype(jnp.bfloat16)
    logits = jnp.dot(normed, router, preferred_element_type=jnp.float32)
    labels = jnp.arange(experts, dtype=jnp.int32)
    first_hot = routes[:, 0][None, :] == labels[:, None]
    second_hot = routes[:, 1][None, :] == labels[:, None]
    first_logit = jnp.sum(jnp.where(first_hot.T, logits, 0.0), axis=1)
    second_logit = jnp.sum(jnp.where(second_hot.T, logits, 0.0), axis=1)
    gate_first = 1.0 / (1.0 + jnp.exp(second_logit - first_logit))
    gate_second = 1.0 / (1.0 + jnp.exp(first_logit - second_logit))
    gates = jnp.where(
        first_hot, gate_first[None, :], jnp.where(second_hot, gate_second[None, :], 0.0)
    )
    named = first_hot | second_hot
    ranking = jnp.cumsum(named.astype(jnp.int32), axis=1) - 1
    chosen = named[:, None, :] & (
        ranking[:, None, :] == jnp.arange(capacity, dtype=jnp.int32)[None, :, None]
    )
    slot_row = jnp.sum(
        jnp.where(chosen, jnp.arange(tok_rows, dtype=jnp.int32)[None, None, :], 0), axis=-1
    )
    filled = jnp.any(chosen, axis=-1)
    picked = jnp.where(filled[..., None], normed[slot_row], jnp.zeros((), jnp.bfloat16))
    outgoing = jnp.broadcast_to(picked[:, None], (experts, blocks, capacity, model_width)).reshape(
        mp_count, capacity, model_width
    )
    places = jnp.where(filled, (device * tok_rows + slot_row) % prompt_len, 0)
    outgoing_places = jnp.broadcast_to(places[:, None], (experts, blocks, capacity)).reshape(
        mp_count, capacity
    )
    arrived = lax.all_to_all(outgoing, "mp", split_axis=0, concat_axis=0, tiled=True)
    arrived_places = lax.all_to_all(outgoing_places, "mp", split_axis=0, concat_axis=0, tiled=True)
    segment = lax.all_gather(normed, "mp", axis=0, tiled=True)
    projected = jnp.dot(segment, pair_w, preferred_element_type=jnp.float32)
    row_places = jnp.arange(segment.shape[0], dtype=jnp.int32) % prompt_len
    keyed = rotate(
        projected[:, :block_width].reshape(-1, block_heads, head_dim), row_places
    ).reshape(-1, block_width)
    kv_rows = jnp.concatenate([keyed, projected[:, block_width:]], axis=1).astype(jnp.bfloat16)
    own_pages = lax.dynamic_slice_in_dim(
        kv_rows, expert * writer_pages * PAGE, writer_pages * PAGE, 0
    )
    own_pages = own_pages.reshape(writer_pages, PAGE, 2 * block_width)
    page_ids = page_table[0, 0]
    target_cells = page_ids // slot_count * PCAP + page_ids % PCAP
    placing = (
        target_cells[None, :] == jnp.arange(mp_count * PCAP, dtype=jnp.int32)[:, None]
    ).astype(jnp.bfloat16)
    outgoing_pages = jnp.einsum(
        "cq,qpk->cpk", placing, own_pages, preferred_element_type=jnp.float32
    ).astype(jnp.bfloat16)
    outgoing_pages = outgoing_pages.reshape(mp_count, PCAP, PAGE, 2 * block_width)
    page_pool = lax.all_to_all(outgoing_pages, "mp", split_axis=0, concat_axis=0, tiled=True)
    queries = jnp.dot(arrived.reshape(-1, model_width), query_w, preferred_element_type=jnp.float32)
    query_places = arrived_places.reshape(-1)
    queries = (
        rotate(queries.reshape(-1, block_heads, head_dim), query_places) * head_dim ** (-0.5)
    ).astype(jnp.bfloat16)
    key_side = (
        kv_rows[:, :block_width].reshape(2, prompt_len, block_heads, head_dim).transpose(0, 2, 1, 3)
    )
    value_side = (
        kv_rows[:, block_width:].reshape(2, prompt_len, block_heads, head_dim).transpose(0, 2, 1, 3)
    )
    key_index = jnp.arange(prompt_len, dtype=jnp.int32)
    half_rows = mp_count // 2 * capacity
    sides = []
    for side in range(2):
        side_places = query_places[side * half_rows : (side + 1) * half_rows]
        length = prompt_lengths[2 * prompt_group + side]
        allowed = (key_index[None, :] <= side_places[:, None]) & (key_index[None, :] < length)
        side_queries = queries[side * half_rows : (side + 1) * half_rows].transpose(1, 0, 2)

        def one_head(operands):
            query_head, key_head, value_head = operands
            scores = lax.dot_general(
                query_head, key_head, (((1,), (1,)), ((), ())), preferred_element_type=jnp.float32
            )
            scores = jnp.where(allowed, scores, -jnp.inf)
            highest = jnp.max(scores, axis=-1, keepdims=True)
            powered = jnp.exp(scores - highest)
            softened = (powered / jnp.sum(powered, axis=-1, keepdims=True)).astype(jnp.bfloat16)
            return jnp.dot(softened, value_head, preferred_element_type=jnp.float32).astype(
                jnp.bfloat16
            )

        sides.append(lax.map(one_head, (side_queries, key_side[side], value_side[side])))
    heads_out = jnp.stack(sides).transpose(0, 2, 1, 3).reshape(2 * half_rows, block_width)
    partial_value = lax.dot_general(
        heads_out, output_w, (((1,), (1,)), ((), ())), preferred_element_type=jnp.float32
    )
    partial_value = partial_value.astype(jnp.bfloat16).reshape(mp_count, capacity, model_width)
    returned = lax.all_to_all(partial_value, "mp", split_axis=0, concat_axis=0, tiled=True)
    page_pool = page_pool.reshape(slot_count, PAGE, 2 * block_width)
    summed = (
        returned.astype(jnp.float32).reshape(experts, blocks, capacity, model_width).sum(axis=1)
    )
    summed = summed.reshape(experts * capacity, model_width)
    weights = jnp.where(chosen, gates[:, None, :], 0.0).reshape(experts * capacity, tok_rows)
    mixed = lax.dot_general(
        weights,
        summed,
        (((0,), (0,)), ((), ())),
        precision=lax.Precision.HIGHEST,
        preferred_element_type=jnp.float32,
    )
    return (mixed.astype(jnp.bfloat16), page_pool)


def solution(mesh):
    placed = (
        P(("dp", "mp"), None),
        P(),
        P(),
        P(("dp", "mp"), None),
        P(),
        P(None, ("dp", "mp"), None),
        P(None, ("dp", "mp"), None),
        P(("dp", "mp"), None),
        P("dp", "mp", None),
    )
    return jax.shard_map(
        on_device,
        mesh=mesh,
        in_specs=placed,
        out_specs=(P(("dp", "mp"), None), P(("dp", "mp"), None, None)),
        check_vma=False,
    )
```

profile of v0, /device:TPU:9, one launch (start us, length us, event | category | flops | bytes accessed | tf_op | source)
XLA Modules:
  0.0 567.2 jit_solution(986742737802211337)
XLA Ops:
  7.2 2.5 convert_element_type.76
  9.7 51.9 %all_to_all.57 = bf16[8,64,2048]{2,1,0:T(8,128)(2,1)S(1)} all-to-all(bf16[8,64,2048]{2,1,0:T(8,128)(2,1)S(1)} %convert_element_type.76), channel_id=1, replica_groups=mesh['dp'=4,'mp'=8] {'mp'}, dimensions={0} | all-to-all | bytes 4194304 | tf_op jit(solution)/shard_map/all_to_all | solution.py:53
  61.6 2.5 copy.28
  67.9 5.7 all-to-all-start.3
  74.8 124.5 %all-to-all-done.3 = bf16[8,64,4096]{2,1,0:T(8,128)(2,1)} async-done(((bf16[8,64,4096]{2,1,0:T(8,128)(2,1)}), bf16[8,64,4096]{2,1,0:T(8,128)(2,1)}, u32[]{:S(2)}, u32[]{:S(2)}) %all-to-all-start.3) | async-done | bytes 4194336 | tf_op jit(solution)/shard_map/all_to_all | solution.py:55
  200.7 6.0 %all-to-all-start.2 = ((s32[8,1,40]{2,1,0:T(1,128)}), s32[8,1,40]{2,1,0:T(1,128)S(1)}, u32[]{:S(2)}, u32[]{:S(2)}) async-start(s32[8,1,40]{2,1,0:T(1,128)} %bitcast.12), calls=%async_computation.2 | async-start | bytes 8192 | tf_op jit(solution)/shard_map/all_to_all | solution.py:100
  206.7 3.8 convert_element_type.82
  210.9 5.2 all-to-all-start.4
  216.2 3.0 gather_fusion
  219.3 2.5 broadcast_select_fusion
  221.8 39.7 %all-to-all-done.4 = bf16[8,64,2048]{2,1,0:T(8,128)(2,1)S(1)} async-done(((bf16[8,64,2048]{2,1,0:T(8,128)(2,1)}), bf16[8,64,2048]{2,1,0:T(8,128)(2,1)S(1)}, u32[]{:S(2)}, u32[]{:S(2)}) %all-to-all-start.4) | async-done | bytes 2097184 | tf_op jit(solution)/shard_map/all_to_all | solution.py:54
  261.5 6.6 %all-to-all-start = ((bf16[8,40,2048]{2,1,0:T(8,128)(2,1)}), bf16[8,40,2048]{2,1,0:T(8,128)(2,1)}, u32[]{:S(2)}, u32[]{:S(2)}) async-start(bf16[8,40,2048]{2,1,0:T(8,128)(2,1)} %broadcast_select_fusion), calls=%async_computation | async-start | bytes 2621440 | tf_op jit(solution)/shard_map/all_to_all | solution.py:99
  270.3 3.0 multiply_cosine_fusion
  274.2 22.4 %all-to-all-done = bf16[8,40,2048]{2,1,0:T(8,128)(2,1)} async-done(((bf16[8,40,2048]{2,1,0:T(8,128)(2,1)}), bf16[8,40,2048]{2,1,0:T(8,128)(2,1)}, u32[]{:S(2)}, u32[]{:S(2)}) %all-to-all-start) | async-done | bytes 1310752 | tf_op jit(solution)/shard_map/all_to_all | solution.py:99
  296.7 5.7 %fusion.72 = f32[320,16,128]{2,0,1:T(8,128)S(1)} fusion(bf16[320,2048,1]{1,0,2:T(8,128)(2,1)} %bitcast.5, bf16[16,128,2048]{2,1,0:T(8,128)(2,1)} %bitcast.168), kind=kOutput, calls=%fused_computation.142 | convolution fusion | flops 2684354560 | bytes 12320768 | tf_op jit(solution)/shard_map/dot_general | solution.py:122
  305.6 19.5 %all-gather.9.cloned.1.call-done = bf16[1,2048,4096]{2,1,0:T(8,128)(2,1)} async-done(((bf16[1,512,4096]{2,1,0:T(8,128)(2,1)}), bf16[1,2048,4096]{2,1,0:T(8,128)(2,1)}) %all-gather.9.cloned.1.call-update) | async-done | bytes 16777232 | tf_op jit(solution)/shard_map/all_gather | solution.py:60
  325.0 23.4 %fusion.32 = f32[1024,4096]{1,0:T(8,128)} fusion(bf16[1024,2048]{1,0:T(8,128)(2,1)} %all-gather.7.cloned.1.call-done, bf16[1,2048,4096]{2,1,0:T(8,128)(2,1)} %all-gather.9.cloned.1.call-done), kind=kOutput, calls=%fused_computation.41 | convolution fusion | flops 17179869184 | bytes 37748736 | tf_op jit(solution)/shard_map/dot_general | solution.py:102
  348.5 4.1 slice_bitcast_fusion
  352.5 4.4 slice_bitcast_fusion.9
  358.9 4.4 subtract_convert_fusion
  374.4 42.7 %while.22 = (s32[]{:T(128)}, bf16[16,160,128]{2,1,0:T(8,128)(2,1)S(1)}, bf16[16,160,128]{2,1,0:T(8,128)(2,1)}, bf16[16,512,128]{2,1,0:T(8,128)(2,1)}, bf16[16,51...) while((s32[]{:T(128)}, ...), condition=%wide.region_9.10_spmd.clone, body=%wide.region_6.9_spmd.clone.sunk | while | flops 42700480 | bytes 1334357 | solution.py:155
  419.1 42.7 %while.23 = (s32[]{:T(128)}, bf16[16,160,128]{2,1,0:T(8,128)(2,1)S(1)}, bf16[16,160,128]{2,1,0:T(8,128)(2,1)}, bf16[16,512,128]{2,1,0:T(8,128)(2,1)}, bf16[16,51...) while((s32[]{:T(128)}, ...), condition=%wide.region_13.14_spmd.clone, body=%wide.region_10.13_spmd.clone.sunk | while | flops 42700480 | bytes 1334357 | solution.py:155
  462.5 7.4 %fusion.36 = bf16[320,2048]{1,0:T(8,128)(2,1)} fusion(bf16[1,2048,2048]{2,1,0:T(8,128)(2,1)} %all-gather.11.cloned.1.call-done, bf16[40,8,16,128]{3,2,1,0:T(8,128)(2,1)S(1)} %bitcast.167), kind=kOutput, calls=%fused_computation.55 | convolution fusion | flops 2685009920 | bytes 11010048 | tf_op jit(solution)/shard_map/dot_general | solution.py:157
  469.9 5.9 %all-to-all-start.5 = ((bf16[8,40,2048]{2,1,0:T(8,128)(2,1)}), bf16[8,40,2048]{2,1,0:T(8,128)(2,1)}, u32[]{:S(2)}, u32[]{:S(2)}) async-start(bf16[8,40,2048]{2,1,0:T(8,128)(2,1)} %bitcast.32), calls=%async_computation.5 | async-start | bytes 2621440 | tf_op jit(solution)/shard_map/all_to_all | solution.py:161
  475.8 4.2 slice.107
  484.0 2.6 reshape.489
  486.6 5.6 copy.35
  492.2 13.1 %all-to-all-done.5 = bf16[8,40,2048]{2,1,0:T(8,128)(2,1)} async-done(((bf16[8,40,2048]{2,1,0:T(8,128)(2,1)}), bf16[8,40,2048]{2,1,0:T(8,128)(2,1)}, u32[]{:S(2)}, u32[]{:S(2)}) %all-to-all-start.5) | async-done | bytes 1310752 | tf_op jit(solution)/shard_map/all_to_all | solution.py:161
  505.4 5.7 all-to-all-start.6
  511.3 3.2 fusion.40
  514.5 43.1 %all-to-all-done.6 = bf16[8,2,16,4096]{3,1,2,0:T(2,128)(2,1)S(1)} async-done(((bf16[8,2,16,4096]{3,1,2,0:T(2,128)(2,1)}), bf16[8,2,16,4096]{3,1,2,0:T(2,128)(2,1)S(1)}, u32[]{:S(2)}, u32[]{:S(2)}) %all-to-all-start.6) | async-done | bytes 2097184 | tf_op jit(solution)/shard_map/all_to_all | solution.py:121
  557.5 2.6 copy.36
  (178 shorter events, 117.7 us)
Async XLA Ops:
  7.2 503.9 %copy-start = (bf16[2048,8]{0,1:T(8,128)(2,1)S(1)}, bf16[2048,8]{0,1:T(8,128)(2,1)}, u32[]{:S(2)}) copy-start(bf16[2048,8]{0,1:T(8,128)(2,1)} %param.15) | copy-start | bytes 98308
  7.2 289.5 %all-gather.5.cloned.1.call-start = ((), (), s32[]{:S(2)}) async-start(), calls=%async_computation.7 | async-start | bytes 10485760 | tf_op jit(solution)/shard_map/all_gather | solution.py:58
  64.1 1.2 copy-start.6
  67.9 5.7 copy-start.5
  67.9 5.9 %copy-start.7 = (f32[2048]{0:T(1024)S(1)}, f32[2048]{0:T(1024)}, u32[]{:S(2)}) copy-start(f32[2048]{0:T(1024)} %param.14) | copy-start | bytes 24580
  67.9 131.4 %all-to-all-start.3 = ((bf16[8,64,4096]{2,1,0:T(8,128)(2,1)}), bf16[8,64,4096]{2,1,0:T(8,128)(2,1)}, u32[]{:S(2)}, u32[]{:S(2)}) async-start(bf16[8,64,4096]{2,1,0:T(8,128)(2,1)} %reshape.481), calls=%async_computation.3 | async-start | bytes 8388608 | tf_op jit(solution)/shard_map/all_to_all | solution.py:55
  73.5 232.0 %all-gather.7.cloned.1.call-start = ((), (), s32[]{:S(2)}) async-start(), calls=%async_computation.8 | async-start | bytes 4718592 | tf_op jit(solution)/shard_map/all_gather | solution.py:101
  74.7 124.6 %copy-start.9 = (s32[128,2]{0,1:T(2,128)S(1)}, s32[128,2]{0,1:T(2,128)}, u32[]{:S(2)}) copy-start(s32[128,2]{0,1:T(2,128)} %param.16) | copy-start | bytes 3076
  74.7 250.3 %all-gather.9.cloned.1.call-start = ((), (), s32[]{:S(2)}) async-start(), calls=%async_computation.9 | async-start | bytes 20971520 | tf_op jit(solution)/shard_map/all_gather | solution.py:60
  200.7 10.3 %all-to-all-start.2 = ((s32[8,1,40]{2,1,0:T(1,128)}), s32[8,1,40]{2,1,0:T(1,128)S(1)}, u32[]{:S(2)}, u32[]{:S(2)}) async-start(s32[8,1,40]{2,1,0:T(1,128)} %bitcast.12), calls=%async_computation.2 | async-start | bytes 8192 | tf_op jit(solution)/shard_map/all_to_all | solution.py:100
  210.6 5.7 %copy-start.1 = (bf16[128,2048]{1,0:T(8,128)(2,1)S(1)}, bf16[128,2048]{1,0:T(8,128)(2,1)}, u32[]{:S(2)}) copy-start(bf16[128,2048]{1,0:T(8,128)(2,1)} %fusion.46) | copy-start | bytes 1572868
  210.9 50.6 %all-to-all-start.4 = ((bf16[8,64,2048]{2,1,0:T(8,128)(2,1)}), bf16[8,64,2048]{2,1,0:T(8,128)(2,1)S(1)}, u32[]{:S(2)}, u32[]{:S(2)}) async-start(bf16[8,64,2048]{2,1,0:T(8,128)(2,1)} %convert_element_type.82), calls=%async_computation.4 | async-start | bytes 4194304 | tf_op jit(solution)/shard_map/all_to_all | solution.py:54
  219.3 49.1 %copy-start.8 = (s32[8]{0:T(128)S(1)}, s32[8]{0:T(128)}, u32[]{:S(2)}) copy-start(s32[8]{0:T(128)} %param.17) | copy-start | bytes 100
  261.5 12.7 %copy-start.4 = (bf16[8,64,2048]{2,1,0:T(8,128)(2,1)}, bf16[8,64,2048]{2,1,0:T(8,128)(2,1)S(1)}, u32[]{:S(2)}) copy-start(bf16[8,64,2048]{2,1,0:T(8,128)(2,1)S(1)} %all-to-all-done.4) | copy-start | bytes 6291460
  261.5 35.1 %all-to-all-start = ((bf16[8,40,2048]{2,1,0:T(8,128)(2,1)}), bf16[8,40,2048]{2,1,0:T(8,128)(2,1)}, u32[]{:S(2)}, u32[]{:S(2)}) async-start(bf16[8,40,2048]{2,1,0:T(8,128)(2,1)} %broadcast_select_fusion), calls=%async_computation | async-start | bytes 2621440 | tf_op jit(solution)/shard_map/all_to_all | solution.py:99
  268.2 194.3 %all-gather.11.cloned.1.call-start = ((), (), s32[]{:S(2)}) async-start(), calls=%async_computation.10 | async-start | bytes 10485760 | tf_op jit(solution)/shard_map/all_gather | solution.py:59
  365.6 1.9 copy-start.2
  469.9 5.9 %copy-start.10 = (s32[1,1,8]{2,1,0:T(1,128)S(1)}, s32[1,1,8]{2,1,0:T(1,128)}, u32[]{:S(2)}) copy-start(s32[1,1,8]{2,1,0:T(1,128)} %param.21) | copy-start | bytes 100
  469.9 35.5 %all-to-all-start.5 = ((bf16[8,40,2048]{2,1,0:T(8,128)(2,1)}), bf16[8,40,2048]{2,1,0:T(8,128)(2,1)}, u32[]{:S(2)}, u32[]{:S(2)}) async-start(bf16[8,40,2048]{2,1,0:T(8,128)(2,1)} %bitcast.32), calls=%async_computation.5 | async-start | bytes 2621440 | tf_op jit(solution)/shard_map/all_to_all | solution.py:161
  475.8 4.6 copy-start.3
  505.4 52.2 %all-to-all-start.6 = ((bf16[8,2,16,4096]{3,1,2,0:T(2,128)(2,1)}), bf16[8,2,16,4096]{3,1,2,0:T(2,128)(2,1)S(1)}, u32[]{:S(2)}, u32[]{:S(2)}) async-start(bf16[8,2,16,4096]{3,1,2,0:T(2,128)(2,1)} %copy.35), calls=%async_computation.6 | async-start | bytes 4194304 | tf_op jit(solution)/shard_map/all_to_all | solution.py:121
Sparse Core Ops, SparseCore 0:
  64.3 59.5 all-gather.4
  126.6 89.4 all-gather.6
  217.7 107.3 all-gather.8
  327.0 58.2 all-gather.10
where the time goes:
time: 576 us; the launch traced here: 567 us
  waiting for transfers between devices  263 us (46%)
  matrix products  119 us (21%)
  blocking collectives  51.9 us (9%)
  local copies, waits for them, and re-layouts  50.5 us (9%)
  starting transfers between devices  35.3 us (6%)
  other arithmetic  32.3 us (6%)
  between operations  14.5 us (3%)
    all_to_all x1, waiting for transfers between devices, on_device(): lax.all_to_all(pair_part, 'mp', split_axis=0, concat_axis=1, tiled=True)  124 us
    all_to_all x1, blocking collectives, on_device(): lax.all_to_all(query_part, 'mp', split_axis=0, concat_axis=1, tiled=True)  51.9 us
    all_to_all x1, waiting for transfers between devices, on_device(): lax.all_to_all(outgoing_pages, 'mp', split_axis=0, concat_axis=0, tiled=T...  43.1 us
    dot_general x32, matrix products, one_head(): lax.dot_general(query_head, key_head, (((1,), (1,)), ((), ())), preferred...  39.8 us
    all_to_all x1, waiting for transfers between devices, on_device(): lax.all_to_all(output_part, 'mp', split_axis=0, concat_axis=1, tiled=True)  39.7 us
    dot_general x32, matrix products, one_head(): jnp.dot(softened, value_head, preferred_element_type=jnp.float32)  37.8 us
    dot_general x1, matrix products, on_device(): projected = jnp.dot(segment, pair_w, preferred_element_type=jnp.float32)  23.4 us
    all_to_all x1, waiting for transfers between devices, on_device(): lax.all_to_all(outgoing, 'mp', split_axis=0, concat_axis=0, tiled=True)  22.4 us
  transfers between devices with their start and end apart: 10, of which 7 were waited for; matrix products, arithmetic and copies ran while one was open for 32% of the time, Pallas kernels for 0%

commit v1 on v0

--- a/solution.py
+++ b/solution.py
@@ -1,6 +1,10 @@
+import functools
+
 import jax
 import jax.numpy as jnp
 from jax import lax
+from jax.experimental import pallas as pl
+from jax.experimental.pallas import tpu as pltpu
 from jax.sharding import PartitionSpec as P
 
 HD = 128
@@ -21,7 +25,7 @@
     )
 
 
-def on_device(
+def by_expert(
     tokens, norm_gain, router, routes, prompt_lengths, wq_train, wo_train, wkv_train, page_table
 ):
     mp_count = lax.axis_size("mp")
@@ -80,7 +84,15 @@
         first_hot, gate_first[None, :], jnp.where(second_hot, gate_second[None, :], 0.0)
     )
     named = first_hot | second_hot
-    ranking = jnp.cumsum(named.astype(jnp.int32), axis=1) - 1
+    upto = jnp.arange(tok_rows)[:, None] <= jnp.arange(tok_rows)[None, :]
+    ranking = (
+        jnp.dot(
+            named.astype(jnp.bfloat16),
+            upto.astype(jnp.bfloat16),
+            preferred_element_type=jnp.float32,
+        ).astype(jnp.int32)
+        - 1
+    )
     chosen = named[:, None, :] & (
         ranking[:, None, :] == jnp.arange(capacity, dtype=jnp.int32)[None, :, None]
     )
@@ -175,6 +187,182 @@
     return (mixed.astype(jnp.bfloat16), page_pool)
 
 
+def turned(vectors, cosine, sine):
+    return vectors * cosine + pltpu.roll(vectors, vectors.shape[-1] // 2, 1) * sine
+
+
+def pages_kernel(heads, source_ref, raw_ref, cosine_ref, sine_ref, kv_ref, pool_ref):
+    rows = raw_ref.shape[0]
+    width = heads * HD
+    for h in range(heads):
+        columns = slice(h * HD, (h + 1) * HD)
+        kv_ref[:, columns] = turned(
+            raw_ref[:, columns], cosine_ref[...], sine_ref[...]
+        ).astype(jnp.bfloat16)
+    kv_ref[:, width:] = raw_ref[:, width:].astype(jnp.bfloat16)
+
+    def place(cell, carry):
+        page = source_ref[cell]
+        start = pl.multiple_of(jnp.maximum(page, 0) * PAGE, PAGE)
+        content = kv_ref[pl.ds(start, PAGE), :]
+        pool_ref[pl.ds(pl.multiple_of(cell * PAGE, PAGE), PAGE), :] = jnp.where(
+            page >= 0, content, jnp.zeros_like(content)
+        )
+        return carry
+
+    lax.fori_loop(0, pool_ref.shape[0] // PAGE, place, 0)
+
+
+def attention_kernel(
+    experts, length_ref, raw_ref, key_ref, value_ref, cosine_ref, sine_ref, side_ref, out_ref
+):
+    rows = key_ref.shape[0]
+    length = length_ref[pl.program_id(0)]
+    key_index = lax.broadcasted_iota(jnp.int32, (rows, rows), 1)
+    row_index = lax.broadcasted_iota(jnp.int32, (rows, rows), 0)
+    allowed = (key_index <= row_index) & (key_index < length)
+    keys = key_ref[...]
+    values = value_ref[...]
+    mixed = []
+    names = []
+    for choice in range(2):
+        name = side_ref[:, choice : choice + 1]
+        gate = side_ref[:, 2 + choice : 3 + choice]
+        query = jnp.zeros((rows, HD), jnp.float32)
+        for e in range(experts):
+            query = jnp.where(name == float(e), raw_ref[:, e * HD : (e + 1) * HD], query)
+        query = (turned(query, cosine_ref[...], sine_ref[...]) * HD ** (-0.5)).astype(jnp.bfloat16)
+        scores = lax.dot_general(
+            query, keys, (((1,), (1,)), ((), ())), preferred_element_type=jnp.float32
+        )
+        scores = jnp.where(allowed, scores, -jnp.inf)
+        highest = jnp.max(scores, axis=-1, keepdims=True)
+        powered = jnp.exp(scores - highest)
+        softened = (powered / jnp.sum(powered, axis=-1, keepdims=True)).astype(jnp.bfloat16)
+        head = jnp.dot(softened, values, preferred_element_type=jnp.float32).astype(jnp.bfloat16)
+        mixed.append((head.astype(jnp.float32) * gate))
+        names.append(name)
+    for e in range(experts):
+        out_ref[:, e * HD : (e + 1) * HD] = jnp.where(
+            names[0] == float(e), mixed[0], jnp.where(names[1] == float(e), mixed[1], 0.0)
+        ).astype(jnp.bfloat16)
+
+
+def by_head(
+    tokens, norm_gain, router, routes, prompt_lengths, wq_train, wo_train, wkv_train, page_table
+):
+    mp_count = lax.axis_size("mp")
+    experts, shard_rows, width = wq_train.shape
+    heads = width // HD // mp_count
+    own_width = heads * HD
+    tok_rows, model_width = tokens.shape
+    group_rows = tok_rows * mp_count
+    prompt_len = group_rows // 2
+    prompt_group = lax.axis_index("dp")
+
+    wide_tokens = tokens.astype(jnp.float32)
+    normed = (
+        wide_tokens
+        * lax.rsqrt(jnp.mean(wide_tokens * wide_tokens, axis=-1, keepdims=True) + 1e-06)
+        * norm_gain
+    ).astype(jnp.bfloat16)
+    segment = lax.all_gather(normed, "mp", axis=0, tiled=True)
+    logits = jnp.dot(normed, router, preferred_element_type=jnp.float32)
+    labels = jnp.arange(experts, dtype=jnp.int32)[None, :]
+    first_logit = jnp.sum(jnp.where(routes[:, 0:1] == labels, logits, 0.0), axis=1)
+    second_logit = jnp.sum(jnp.where(routes[:, 1:2] == labels, logits, 0.0), axis=1)
+    gate_first = 1.0 / (1.0 + jnp.exp(second_logit - first_logit))
+    gate_second = 1.0 / (1.0 + jnp.exp(first_logit - second_logit))
+    side = jnp.concatenate(
+        [routes.astype(jnp.float32), gate_first[:, None], gate_second[:, None]], axis=1
+    )
+    side = lax.all_gather(side, "mp", axis=0, tiled=True)
+    page_ids = lax.all_gather(page_table[0, 0], "mp", axis=0, tiled=True)
+
+    def by_owner(weights):
+        parts = weights.astype(jnp.bfloat16).reshape(experts, shard_rows, mp_count, heads, HD)
+        return parts.transpose(2, 1, 3, 0, 4).reshape(mp_count, shard_rows, experts * own_width)
+
+    pair = wkv_train.astype(jnp.bfloat16).reshape(shard_rows, 2, mp_count, own_width)
+    pair = pair.transpose(2, 0, 1, 3).reshape(mp_count, shard_rows, 2 * own_width)
+    inward = jnp.concatenate([by_owner(wq_train), pair], axis=2)
+    inward = lax.all_to_all(inward, "mp", split_axis=0, concat_axis=0, tiled=True)
+    inward = lax.all_gather(
+        inward.reshape(mp_count * shard_rows, -1), "dp", axis=0, tiled=True
+    )
+    outward = lax.all_to_all(by_owner(wo_train), "mp", split_axis=0, concat_axis=0, tiled=True)
+    outward = lax.all_gather(
+        outward.reshape(mp_count * shard_rows, -1), "dp", axis=0, tiled=True
+    )
+
+    projected = jnp.dot(segment, inward, preferred_element_type=jnp.float32)
+
+    half = HD // 2
+    frequency = 10000.0 ** (-(jnp.arange(half, dtype=jnp.float32) * 2.0 / HD))
+    angles = jnp.arange(prompt_len, dtype=jnp.float32)[:, None] * frequency[None, :]
+    cosine = jnp.concatenate([jnp.cos(angles)] * 2, axis=1)
+    sine = jnp.concatenate([-jnp.sin(angles), jnp.sin(angles)], axis=1)
+
+    cells = jnp.arange(mp_count * mp_count * PCAP, dtype=jnp.int32)
+    pages = jnp.arange(page_ids.shape[0], dtype=jnp.int32)
+    source = jnp.sum(jnp.where(page_ids[None, :] == cells[:, None], pages[None, :] + 1, 0), 1) - 1
+    query_width = experts * own_width
+    key_values, pool = pl.pallas_call(
+        functools.partial(pages_kernel, heads),
+        grid=(1,),
+        in_specs=[
+            pl.BlockSpec(memory_space=pltpu.SMEM),
+            pl.BlockSpec((group_rows, 2 * own_width), lambda i: (0, query_width // (2 * own_width))),
+            pl.BlockSpec((group_rows, HD), lambda i: (0, 0)),
+            pl.BlockSpec((group_rows, HD), lambda i: (0, 0)),
+        ],
+        out_specs=[
+            pl.BlockSpec((group_rows, 2 * own_width), lambda i: (0, 0)),
+            pl.BlockSpec((cells.shape[0] * PAGE, 2 * own_width), lambda i: (0, 0)),
+        ],
+        out_shape=[
+            jax.ShapeDtypeStruct((group_rows, 2 * own_width), jnp.bfloat16),
+            jax.ShapeDtypeStruct((cells.shape[0] * PAGE, 2 * own_width), jnp.bfloat16),
+        ],
+        compiler_params=pltpu.CompilerParams(vmem_limit_bytes=40 * 2**20),
+    )(source, projected, jnp.concatenate([cosine] * 2), jnp.concatenate([sine] * 2))
+    pool = pool.reshape(mp_count, mp_count * PCAP, PAGE, 2 * own_width)
+    pool = lax.all_to_all(pool, "mp", split_axis=0, concat_axis=0, tiled=True)
+    pool = pool.reshape(mp_count, mp_count * PCAP, PAGE, 2, own_width).transpose(1, 2, 3, 0, 4)
+    pool = pool.reshape(mp_count * PCAP, PAGE, 2 * width)
+
+    lengths = lax.dynamic_slice_in_dim(prompt_lengths, 2 * prompt_group, 2)
+    head_width = experts * HD
+    mixed = pl.pallas_call(
+        functools.partial(attention_kernel, experts),
+        grid=(2, heads),
+        in_specs=[
+            pl.BlockSpec(memory_space=pltpu.SMEM),
+            pl.BlockSpec((prompt_len, head_width), lambda p, h: (p, h)),
+            pl.BlockSpec((prompt_len, HD), lambda p, h: (p, h)),
+            pl.BlockSpec((prompt_len, HD), lambda p, h: (p, heads + h)),
+            pl.BlockSpec((prompt_len, HD), lambda p, h: (0, 0)),
+            pl.BlockSpec((prompt_len, HD), lambda p, h: (0, 0)),
+            pl.BlockSpec((prompt_len, side.shape[1]), lambda p, h: (p, 0)),
+        ],
+        out_specs=pl.BlockSpec((prompt_len, head_width), lambda p, h: (p, h)),
+        out_shape=jax.ShapeDtypeStruct((group_rows, heads * head_width), jnp.bfloat16),
+        compiler_params=pltpu.CompilerParams(vmem_limit_bytes=40 * 2**20),
+    )(lengths, projected, key_values, key_values, cosine, sine, side)
+    partial_value = lax.dot_general(
+        mixed, outward, (((1,), (1,)), ((), ())), preferred_element_type=jnp.float32
+    ).astype(jnp.bfloat16)
+    attended = lax.psum_scatter(partial_value, "mp", scatter_dimension=0, tiled=True)
+    return (attended, pool)
+
+
+def on_device(tokens, norm_gain, router, routes, prompt_lengths, wq_train, *others):
+    mp_count = lax.axis_size("mp")
+    split_heads = wq_train.shape[0] == mp_count and wq_train.shape[2] // HD % mp_count == 0
+    program = by_head if split_heads else by_expert
+    return program(tokens, norm_gain, router, routes, prompt_lengths, wq_train, *others)
+
+
 def solution(mesh):
     placed = (
         P(("dp", "mp"), None),

time: 576 us -> 422 us (0.73); the launches traced: 567 us -> 419 us
  waiting for transfers between devices: 263 us -> 41.4 us
  blocking collectives: 51.9 us -> 265 us
  matrix products: 119 us -> 31.7 us
  starting transfers between devices: 35.3 us -> 0.16 us
  other arithmetic: 32.3 us -> 11.4 us
  Pallas kernels: 0 us -> 17.5 us
  local copies, waits for them, and re-layouts: 50.5 us -> 37.2 us
    all_to_all x6 -> x0, waiting for transfers between devices: 243 us -> none  [the longest x1 124 us: on_device(): lax.all_to_all(pair_part, 'mp', split_axis=0, concat_axis=1, tiled=True)]
    all_to_all x1 -> x3, blocking collectives: 51.9 us -> 234 us  [the longest x1 104 us: by_head(): lax.all_to_all(inward, 'mp', split_axis=0, concat_axis=0, tiled=True)]
    dot_general x70 -> x3, matrix products: 119 us -> 31.7 us  [the longest x1 17.5 us: by_head(): projected = jnp.dot(segment, inward, preferred_element_type=jnp.float32)]
    reduce_scatter x0 -> x1, waiting for transfers between devices: none -> 41.3 us  [by_head(): lax.psum_scatter(partial_value, 'mp', scatter_dimension=0, tiled=True)]
    all_to_all x6 -> x0, starting transfers between devices: 35.1 us -> none  [the longest x1 6.63 us: on_device(): lax.all_to_all(outgoing, 'mp', split_axis=0, concat_axis=0, tiled=True)]
    all_gather x0 -> x1, blocking collectives: none -> 23.4 us  [by_head(): side = lax.all_gather(side, 'mp', axis=0, tiled=True)]
    reshape x4 -> x11, local copies, waits for them, and re-layouts: 11.8 us -> 31.4 us  [the longest x4 15.1 us: by_owner(): weights.astype(jnp.bfloat16)]
    all_gather x4 -> x3, waiting for transfers between devices: 19.5 us -> 0.04 us  [the longest x1 0.02 us: by_head(): segment = lax.all_gather(normed, 'mp', axis=0, tiled=True)]
  transfers between devices with their start and end apart: 10 -> 4, of which waited for: 7 -> 1; matrix products, arithmetic and copies ran while one was open for 32% -> 14% of each run, Pallas kernels for 0% -> 4%
where the time goes in v1:
time: 422 us; the launch traced here: 419 us
  blocking collectives  265 us (63%)
  waiting for transfers between devices  41.4 us (10%)
  local copies, waits for them, and re-layouts  37.2 us (9%)
  matrix products  31.7 us (8%)
  Pallas kernels  17.5 us (4%)
  between operations  14.7 us (3%)
  other arithmetic  11.4 us (3%)
    all_to_all x1, blocking collectives, by_head(): lax.all_to_all(inward, 'mp', split_axis=0, concat_axis=0, tiled=True)  104 us
    all_to_all x1, blocking collectives, by_head(): pool = lax.all_to_all(pool, 'mp', split_axis=0, concat_axis=0, tiled=True)  78.7 us
    all_to_all x1, blocking collectives, by_head(): lax.all_to_all(by_owner(wo_train), 'mp', split_axis=0, concat_axis=0, til...  51.8 us
    reduce_scatter x1, waiting for transfers between devices, by_head(): lax.psum_scatter(partial_value, 'mp', scatter_dimension=0, tiled=True)  41.3 us
    all_gather x1, blocking collectives, by_head(): side = lax.all_gather(side, 'mp', axis=0, tiled=True)  23.4 us
    dot_general x1, matrix products, by_head(): projected = jnp.dot(segment, inward, preferred_element_type=jnp.float32)  17.5 us
    reshape x4, local copies, waits for them, and re-layouts, by_owner(): weights.astype(jnp.bfloat16)  15.1 us
    pallas_call x1, Pallas kernels, by_head(): pl.pallas_call(functools.partial(attention_kernel, experts), grid=(2, hea...  14.3 us
  transfers between devices with their start and end apart: 4, of which 1 were waited for; matrix products, arithmetic and copies ran while one was open for 14% of the time, Pallas kernels for 4%

profile of v1, /device:TPU:9, one launch (start us, length us, event | category | flops | bytes accessed | tf_op | source)
XLA Modules:
  0.0 419.3 jit_solution(135684089302927520)
XLA Ops:
  7.2 1.2 fusion
  8.5 2.0 fusion.2
  10.6 1.3 convert_element_type.24
  12.0 0.4 copy.40
  12.4 0.3 reshape.113
  12.7 2.5 convert_element_type.23
  15.2 2.7 reshape.110
  17.9 5.4 %copy.39 = bf16[8,64,8,2,128]{4,0,3,1,2:T(8,128)(2,1)} copy(bf16[8,64,8,2,128]{4,3,2,1,0:T(2,128)(2,1)} %reshape.110) | data formatting | bytes 4194304 | tf_op jit(solution)/shard_map/reshape | solution.py:283
  23.3 2.8 reshape.111
  26.3 103.9 %all_to_all.15 = bf16[8,64,2560]{2,1,0:T(8,128)(2,1)} all-to-all(bf16[8,64,2560]{2,1,0:T(8,128)(2,1)S(1)} %pad_maximum_fusion), channel_id=1, replica_groups=mesh['dp'=4,'mp'=8] {'mp'}, dimensions={0} | all-to-all | bytes 5242880 | tf_op jit(solution)/shard_map/all_to_all | solution.py:289
  130.3 2.5 convert_element_type.26
  132.8 2.7 reshape.115
  135.5 4.3 %copy.38 = bf16[8,64,8,2,128]{4,0,3,1,2:T(8,128)(2,1)S(1)} copy(bf16[8,64,8,2,128]{4,3,2,1,0:T(2,128)(2,1)} %reshape.115) | data formatting | bytes 4194304 | tf_op jit(solution)/shard_map/reshape | solution.py:283
  139.8 2.3 reshape.116
  142.1 51.8 %all_to_all.16 = bf16[8,64,2048]{2,1,0:T(8,128)(2,1)} all-to-all(bf16[8,64,2048]{2,1,0:T(8,128)(2,1)} %reshape.116), channel_id=1, replica_groups=mesh['dp'=4,'mp'=8] {'mp'}, dimensions={0} | all-to-all | bytes 4194304 | tf_op jit(solution)/shard_map/all_to_all | solution.py:293
  194.6 0.6 dynamic-slice
  195.9 7.3 %all-reduce = s32[64]{0:T(128)S(1)} all-reduce(s32[64]{0:T(128)S(1)} %bitcast_dynamic-update-slice_fusion), channel_id=2, replica_groups=mesh['dp'=4,'mp'=8] {'mp'}, use_global_device_ids=true, to_apply=%add | all-reduce | flops 64 | bytes 512
  203.3 23.4 %all_gather.18.side_ref = f32[1024,4]{1,0:T(8,128)S(1)} all-gather(f32[128,4]{1,0:T(8,128)S(1)} %copy.29), channel_id=1, replica_groups=mesh['dp'=4,'mp'=8] {'mp'}, dimensions={0}, use_global_device_ids=true | all-gather | bytes 18432 | tf_op jit(solution)/shard_map/all_gather | solution.py:279
  226.8 1.0 fusion.5
  228.0 0.3 maximum_maximum_fusion
  228.4 17.5 %fusion.6.raw_ref = f32[1024,2560]{1,0:T(8,128)} fusion(bf16[1024,2048]{1,0:T(8,128)(2,1)} %all-gather.5.cloned.1.call-done, bf16[2048,2560]{1,0:T(8,128)(2,1)} %all-gather.7.cloned.1.call-done), kind=kOutput, calls=%fused_computation.35 | convolution fusion | flops 10737418240 | bytes 25165824 | tf_op jit(solution)/shard_map/dot_general | solution.py:298
  245.9 3.2 shard_map.104
  249.2 1.3 copy-done.3
  250.5 14.3 %shard_map.105 = bf16[1024,2048]{1,0:T(8,128)(2,1)S(1)} custom-call(s32[2]{0:T(128)S(1)} %dynamic_slice.3.length_ref, f32[1024,2560]{1,0:T(8,128)} %fusion.6.raw_ref, bf16[1024,512]{1,0:T(8,128)(2,1)S(1)} %get-tuple-element.4.key_ref.value_ref, bf16[1024,512]{1,0:T(8,128)(2,1)S(1)} %get-tuple-element.4.key_ref.value_ref, ...), custom_call_target="tpu_custom_call" | custom-call | tf_op jit(solution)/shard_map/pallas_call | solution.py:336
  264.8 2.0 copy-done.2
  266.8 13.9 %convolution_convert_fusion = bf16[1024,2048]{1,0:T(8,128)(2,1)} fusion(bf16[1024,2048]{1,0:T(8,128)(2,1)} %copy-done.2, bf16[2048,2048]{1,0:T(8,128)(2,1)} %all-gather.9.cloned.1.call-done), kind=kOutput, calls=%fused_computation | convolution fusion | flops 8592031744 | bytes 16777216 | tf_op jit(solution)/shard_map/dot_general | solution.py:352
  280.7 1.6 copy-done.4
  282.3 78.7 %all_to_all.17 = bf16[8,16,16,512]{3,2,1,0:T(8,128)(2,1)} all-to-all(bf16[8,16,16,512]{3,2,1,0:T(8,128)(2,1)S(1)} %bitcast.43), channel_id=1, replica_groups=mesh['dp'=4,'mp'=8] {'mp'}, dimensions={0} | all-to-all | bytes 4194304 | tf_op jit(solution)/shard_map/all_to_all | solution.py:330
  361.0 2.6 reshape.119
  363.6 3.7 copy.37
  367.2 4.2 %reshape.120 = bf16[16,16,4096]{2,1,0:T(8,128)(2,1)} reshape(bf16[16,16,2,8,256]{4,3,2,1,0:T(8,128)(2,1)} %bitcast.48) | data formatting | bytes 4194304 | tf_op jit(solution)/shard_map/reshape | solution.py:332
  371.4 41.3 %reduce-scatter.2.cloned.1.call-done = bf16[128,2048]{1,0:T(8,128)(2,1)} async-done(((bf16[1024,2048]{1,0:T(8,128)(2,1)}), bf16[128,2048]{1,0:T(8,128)(2,1)}) %reduce-scatter.2.cloned.1.call-update) | async-done | bytes 524304 | tf_op jit(solution)/shard_map/reduce_scatter | solution.py:355
  (45 shorter events, 1.5 us)
Async XLA Ops:
  7.2 186.9 %copy-start = (bf16[2048,8]{0,1:T(8,128)(2,1)S(1)}, bf16[2048,8]{0,1:T(8,128)(2,1)}, u32[]{:S(2)}) copy-start(bf16[2048,8]{0,1:T(8,128)(2,1)} %param.11) | copy-start | bytes 98308
  7.2 221.2 %all-gather.5.cloned.1.call-start = ((), (), s32[]{:S(2)}) async-start(), calls=%async_computation.4 | async-start | bytes 4718592 | tf_op jit(solution)/shard_map/all_gather | solution.py:269
  10.5 217.8 %all-gather.7.cloned.1.call-start = ((), (), s32[]{:S(2)}) async-start(), calls=%async_computation.5 | async-start | bytes 13107200 | tf_op jit(solution)/shard_map/all_gather | solution.py:290
  130.2 136.5 %all-gather.9.cloned.1.call-start = ((), (), s32[]{:S(2)}) async-start(), calls=%async_computation.6 | async-start | bytes 10485760 | tf_op jit(solution)/shard_map/all_gather | solution.py:294
  142.1 51.9 %copy-start.6 = (s32[128,2]{0,1:T(2,128)S(1)}, s32[128,2]{0,1:T(2,128)}, u32[]{:S(2)}) copy-start(s32[128,2]{0,1:T(2,128)} %param.12) | copy-start | bytes 3076
  142.1 52.0 %copy-start.5 = (bf16[128,2048]{1,0:T(8,128)(2,1)S(1)}, bf16[128,2048]{1,0:T(8,128)(2,1)}, u32[]{:S(2)}) copy-start(bf16[128,2048]{1,0:T(8,128)(2,1)} %fusion.2) | copy-start | bytes 1572868
  142.1 52.4 %copy-start.7 = (s32[8]{0:T(128)S(1)}, s32[8]{0:T(128)}, u32[]{:S(2)}) copy-start(s32[8]{0:T(128)} %param.13) | copy-start | bytes 100
  142.1 52.5 %copy-start.9 = (u32[32]{0:T(128)S(1)}, u32[32]{0:T(128)}, u32[]{:S(2)}) copy-start(u32[32]{0:T(128)} %constant.35) | copy-start | bytes 388
  142.1 53.7 %copy-start.8 = (s32[1,1,8]{2,1,0:T(1,128)S(1)}, s32[1,1,8]{2,1,0:T(1,128)}, u32[]{:S(2)}) copy-start(s32[1,1,8]{2,1,0:T(1,128)} %param.17) | copy-start | bytes 100
  194.0 218.8 %reduce-scatter.2.cloned.1.call-start = ((), (), s32[]{:S(2)}) async-start(), calls=%async_computation.7 | async-start | bytes 4718592 | tf_op jit(solution)/shard_map/reduce_scatter | solution.py:355
  249.2 1.3 copy-start.3
  264.8 2.0 copy-start.2
  280.7 1.6 copy-start.4
  361.0 51.8 %copy-start.1 = (bf16[2048,8]{0,1:T(8,128)(2,1)S(1)}, bf16[2048,8]{0,1:T(8,128)(2,1)}, u32[]{:S(2)}) copy-start(bf16[2048,8]{0,1:T(8,128)(2,1)} %param.11) | copy-start | bytes 98308
Sparse Core Ops, SparseCore 0:
  10.7 111.6 all-gather.4
  130.4 70.1 all-gather.6
  202.1 58.2 all-gather.8
  280.8 131.8 reduce-scatter.1

commit v2 on v1

--- a/solution.py
+++ b/solution.py
@@ -248,6 +248,240 @@
         ).astype(jnp.bfloat16)
 
 
+def pack_kernel(heads, query_ref, output_ref, key_ref, value_ref, inward_ref, outward_ref):
+    experts = query_ref.shape[0]
+    for h in range(heads):
+        for e in range(experts):
+            columns = slice((h * experts + e) * HD, (h * experts + e + 1) * HD)
+            own = slice(h * HD, (h + 1) * HD)
+            inward_ref[0, :, columns] = query_ref[e, :, own].astype(jnp.bfloat16)
+            outward_ref[0, :, columns] = output_ref[e, :, own].astype(jnp.bfloat16)
+    start = heads * experts * HD
+    inward_ref[0, :, start : start + heads * HD] = key_ref[...].astype(jnp.bfloat16)
+    inward_ref[0, :, start + heads * HD :] = value_ref[...].astype(jnp.bfloat16)
+
+
+def greet(peers):
+    barrier = pltpu.get_barrier_semaphore()
+    for peer in peers:
+        pl.semaphore_signal(barrier, inc=1, device_id=peer, device_id_type=pl.DeviceIdType.MESH)
+    pl.semaphore_wait(barrier, len(peers))
+
+
+def exchange_kernel(
+    mp_count,
+    inward_ref,
+    outward_ref,
+    normed_ref,
+    side_ref,
+    table_ref,
+    inward_all,
+    outward_all,
+    normed_all,
+    side_all,
+    table_all,
+    local_sem,
+    send_sem,
+    recv_sem,
+    send_small,
+    recv_small,
+):
+    d = lax.axis_index("dp")
+    m = lax.axis_index("mp")
+    twin = d + 1 - 2 * lax.rem(d, 2)
+    across = lax.rem(d + 2, 4)
+    beside = m + 1 - 2 * lax.rem(m, 2)
+
+    def shifted(k):
+        return lax.rem(m + k + mp_count, mp_count)
+
+    greet([(d, shifted(k)) for k in range(1, mp_count)] + [(twin, m), (across, m)])
+    sent = []
+
+    def send(source, target, sems, place, device):
+        copy = pltpu.make_async_remote_copy(
+            src_ref=source,
+            dst_ref=target,
+            send_sem=sems[0].at[place],
+            recv_sem=sems[1].at[place],
+            device_id=device,
+            device_id_type=pl.DeviceIdType.MESH,
+        )
+        copy.start()
+        sent.append(copy)
+
+    def arrived(target, sems, place):
+        pltpu.make_async_remote_copy(
+            src_ref=target,
+            dst_ref=target,
+            send_sem=sems[0].at[place],
+            recv_sem=sems[1].at[place],
+            device_id=(twin, m),
+            device_id_type=pl.DeviceIdType.MESH,
+        ).wait_recv()
+
+    wide = (send_sem, recv_sem)
+    small = (send_small, recv_small)
+    parts = (inward_ref, outward_ref)
+    wholes = (inward_all, outward_all)
+    lines = mp_count // 2
+    own = d * mp_count + m
+    locals_ = [
+        pltpu.make_async_copy(inward_ref.at[m], inward_all.at[own], local_sem.at[0]),
+        pltpu.make_async_copy(outward_ref.at[m], outward_all.at[own], local_sem.at[1]),
+        pltpu.make_async_copy(normed_ref, normed_all.at[m], local_sem.at[2]),
+        pltpu.make_async_copy(side_ref, side_all.at[m], local_sem.at[3]),
+        pltpu.make_async_copy(table_ref, table_all.at[m], local_sem.at[4]),
+    ]
+    for part in range(2):
+        for k in range(1, mp_count):
+            to = shifted(k)
+            send(parts[part].at[to], wholes[part].at[own], wide, (part, 0, k), (d, to))
+        if part == 0:
+            for k in range(1, lines):
+                send(normed_ref, normed_all.at[m], small, (2, k), (d, shifted(2 * k)))
+            for k in range(1, mp_count):
+                to = shifted(k)
+                send(side_ref, side_all.at[m], small, (0, k), (d, to))
+                send(table_ref, table_all.at[m], small, (1, k), (d, to))
+    for copy in locals_:
+        copy.start()
+
+    def relay(part, k):
+        slot = across * mp_count + shifted(-k)
+        arrived(wholes[part].at[slot], wide, (part, 1, k))
+        send(wholes[part].at[slot], wholes[part].at[slot], wide, (part, 3, k), (twin, m))
+
+    steps = [(part, k) for part in range(2) for k in range(mp_count)]
+    for i, (part, k) in enumerate(steps):
+        slot = d * mp_count + shifted(-k)
+        source = parts[part].at[m]
+        if k > 0:
+            arrived(wholes[part].at[slot], wide, (part, 0, k))
+            source = wholes[part].at[slot]
+        send(source, wholes[part].at[slot], wide, (part, 1, k), (across, m))
+        send(source, wholes[part].at[slot], wide, (part, 2, k), (twin, m))
+        if i >= 2:
+            relay(*steps[i - 2])
+        if part == 0 and k < lines:
+            row = shifted(-2 * k)
+            block = normed_ref
+            if k > 0:
+                arrived(normed_all.at[row], small, (2, k))
+                block = normed_all.at[row]
+            send(block, normed_all.at[row], small, (3, k), (d, beside))
+    relay(*steps[-2])
+    relay(*steps[-1])
+    for part, k in steps:
+        arrived(wholes[part].at[twin * mp_count + shifted(-k)], wide, (part, 2, k))
+        far = lax.rem(twin + 2, 4)
+        arrived(wholes[part].at[far * mp_count + shifted(-k)], wide, (part, 3, k))
+    for k in range(lines):
+        arrived(normed_all.at[lax.rem(beside - 2 * k + mp_count, mp_count)], small, (3, k))
+    for k in range(1, mp_count):
+        arrived(side_all.at[shifted(-k)], small, (0, k))
+        arrived(table_all.at[shifted(-k)], small, (1, k))
+    for copy in sent:
+        copy.wait_send()
+    for copy in locals_:
+        copy.wait()
+
+
+def return_kernel(
+    mp_count,
+    partial_ref,
+    pool_ref,
+    out_ref,
+    pool_all,
+    pair_in,
+    line_out,
+    line_in,
+    local_sem,
+    send_sem,
+    recv_sem,
+    send_page,
+    recv_page,
+):
+    d = lax.axis_index("dp")
+    m = lax.axis_index("mp")
+    line = m // 2
+    x = lax.rem(m, 2)
+    lines = mp_count // 2
+    own_width = pool_ref.shape[2] // 2
+    width = own_width * mp_count
+
+    def shifted(k):
+        return lax.rem(m + k + mp_count, mp_count)
+
+    greet([(d, shifted(k)) for k in range(1, mp_count)])
+    sent = []
+
+    def remote(source, target, sends, receives, place, device):
+        return pltpu.make_async_remote_copy(
+            src_ref=source,
+            dst_ref=target,
+            send_sem=sends.at[place],
+            recv_sem=receives.at[place],
+            device_id=device,
+            device_id_type=pl.DeviceIdType.MESH,
+        )
+
+    def send(*description):
+        copy = remote(*description)
+        copy.start()
+        sent.append(copy)
+
+    beside = (d, line * 2 + 1 - x)
+    for k in [*range(1, lines), 0]:
+        goal = lax.rem(line + k, lines)
+        send(partial_ref.at[goal * 2 + 1 - x], pair_in.at[k], send_sem, recv_sem, (0, k), beside)
+
+    def columns(side, device):
+        return pl.ds(pl.multiple_of(side * width + device * own_width, own_width), own_width)
+
+    locals_ = []
+    for side in range(2):
+        half = pl.ds(side * own_width, own_width)
+        locals_.append(
+            pltpu.make_async_copy(
+                pool_ref.at[m, :, half], pool_all.at[:, columns(side, m)], local_sem.at[side]
+            )
+        )
+        locals_[-1].start()
+        for k in range(1, mp_count):
+            to = shifted(k)
+            send(
+                pool_ref.at[to, :, half],
+                pool_all.at[:, columns(side, m)],
+                send_page,
+                recv_page,
+                (side, k),
+                (d, to),
+            )
+    for k in range(1, lines):
+        goal = lax.rem(line + k, lines)
+        remote(pair_in.at[k], pair_in.at[k], send_sem, recv_sem, (0, k), beside).wait_recv()
+        line_out[k] = (
+            partial_ref[goal * 2 + x].astype(jnp.float32) + pair_in[k].astype(jnp.float32)
+        ).astype(jnp.bfloat16)
+        send(line_out.at[k], line_in.at[k], send_sem, recv_sem, (1, k), (d, goal * 2 + x))
+    remote(pair_in.at[0], pair_in.at[0], send_sem, recv_sem, (0, 0), beside).wait_recv()
+    for k in range(1, lines):
+        remote(line_in.at[k], line_in.at[k], send_sem, recv_sem, (1, k), beside).wait_recv()
+    total = partial_ref[m].astype(jnp.float32) + pair_in[0].astype(jnp.float32)
+    for k in range(1, lines):
+        total = total + line_in[k].astype(jnp.float32)
+    out_ref[...] = total.astype(jnp.bfloat16)
+    for side in range(2):
+        for k in range(1, mp_count):
+            target = pool_all.at[:, columns(side, shifted(-k))]
+            remote(target, target, send_page, recv_page, (side, k), beside).wait_recv()
+    for copy in sent:
+        copy.wait_send()
+    for copy in locals_:
+        copy.wait()
+
+
 def by_head(
     tokens, norm_gain, router, routes, prompt_lengths, wq_train, wo_train, wkv_train, page_table
 ):
@@ -266,7 +500,6 @@
         * lax.rsqrt(jnp.mean(wide_tokens * wide_tokens, axis=-1, keepdims=True) + 1e-06)
         * norm_gain
     ).astype(jnp.bfloat16)
-    segment = lax.all_gather(normed, "mp", axis=0, tiled=True)
     logits = jnp.dot(normed, router, preferred_element_type=jnp.float32)
     labels = jnp.arange(experts, dtype=jnp.int32)[None, :]
     first_logit = jnp.sum(jnp.where(routes[:, 0:1] == labels, logits, 0.0), axis=1)
@@ -276,24 +509,55 @@
     side = jnp.concatenate(
         [routes.astype(jnp.float32), gate_first[:, None], gate_second[:, None]], axis=1
     )
-    side = lax.all_gather(side, "mp", axis=0, tiled=True)
-    page_ids = lax.all_gather(page_table[0, 0], "mp", axis=0, tiled=True)
-
-    def by_owner(weights):
-        parts = weights.astype(jnp.bfloat16).reshape(experts, shard_rows, mp_count, heads, HD)
-        return parts.transpose(2, 1, 3, 0, 4).reshape(mp_count, shard_rows, experts * own_width)
-
-    pair = wkv_train.astype(jnp.bfloat16).reshape(shard_rows, 2, mp_count, own_width)
-    pair = pair.transpose(2, 0, 1, 3).reshape(mp_count, shard_rows, 2 * own_width)
-    inward = jnp.concatenate([by_owner(wq_train), pair], axis=2)
-    inward = lax.all_to_all(inward, "mp", split_axis=0, concat_axis=0, tiled=True)
-    inward = lax.all_gather(
-        inward.reshape(mp_count * shard_rows, -1), "dp", axis=0, tiled=True
-    )
-    outward = lax.all_to_all(by_owner(wo_train), "mp", split_axis=0, concat_axis=0, tiled=True)
-    outward = lax.all_gather(
-        outward.reshape(mp_count * shard_rows, -1), "dp", axis=0, tiled=True
-    )
+    side = jnp.pad(side, ((0, 0), (0, HD - side.shape[1])))
+    table = jnp.pad(page_table[0], ((0, 7), (0, HD - page_table.shape[2])))
+
+    inner = experts * own_width
+    inward, outward = pl.pallas_call(
+        functools.partial(pack_kernel, heads),
+        grid=(mp_count,),
+        in_specs=[
+            pl.BlockSpec((experts, shard_rows, own_width), lambda i: (0, 0, i)),
+            pl.BlockSpec((experts, shard_rows, own_width), lambda i: (0, 0, i)),
+            pl.BlockSpec((shard_rows, own_width), lambda i: (0, i)),
+            pl.BlockSpec((shard_rows, own_width), lambda i: (0, mp_count + i)),
+        ],
+        out_specs=[
+            pl.BlockSpec((1, shard_rows, inner + 2 * own_width), lambda i: (i, 0, 0)),
+            pl.BlockSpec((1, shard_rows, inner), lambda i: (i, 0, 0)),
+        ],
+        out_shape=[
+            jax.ShapeDtypeStruct((mp_count, shard_rows, inner + 2 * own_width), jnp.bfloat16),
+            jax.ShapeDtypeStruct((mp_count, shard_rows, inner), jnp.bfloat16),
+        ],
+        compiler_params=pltpu.CompilerParams(vmem_limit_bytes=32 * 2**20),
+    )(wq_train, wo_train, wkv_train, wkv_train)
+    places = 4 * mp_count
+    inward, outward, segment, side, table = pl.pallas_call(
+        functools.partial(exchange_kernel, mp_count),
+        in_specs=[pl.BlockSpec(memory_space=pl.ANY)] * 5,
+        out_specs=[pl.BlockSpec(memory_space=pl.ANY)] * 5,
+        out_shape=[
+            jax.ShapeDtypeStruct((places, *inward.shape[1:]), jnp.bfloat16),
+            jax.ShapeDtypeStruct((places, *outward.shape[1:]), jnp.bfloat16),
+            jax.ShapeDtypeStruct((mp_count, *normed.shape), jnp.bfloat16),
+            jax.ShapeDtypeStruct((mp_count, *side.shape), jnp.float32),
+            jax.ShapeDtypeStruct((mp_count, *table.shape), jnp.int32),
+        ],
+        scratch_shapes=[
+            pltpu.SemaphoreType.DMA((5,)),
+            pltpu.SemaphoreType.DMA((2, 4, mp_count)),
+            pltpu.SemaphoreType.DMA((2, 4, mp_count)),
+            pltpu.SemaphoreType.DMA((4, mp_count)),
+            pltpu.SemaphoreType.DMA((4, mp_count)),
+        ],
+        compiler_params=pltpu.CompilerParams(collective_id=0, has_side_effects=True),
+    )(inward, outward, normed, side, table)
+    inward = inward.reshape(places * shard_rows, -1)
+    outward = outward.reshape(places * shard_rows, -1)
+    segment = segment.reshape(group_rows, model_width)
+    side = side.reshape(group_rows, HD)
+    page_ids = table[:, 0, : page_table.shape[2]].reshape(-1)
 
     projected = jnp.dot(segment, inward, preferred_element_type=jnp.float32)
 
@@ -326,11 +590,8 @@
         ],
         compiler_params=pltpu.CompilerParams(vmem_limit_bytes=40 * 2**20),
     )(source, projected, jnp.concatenate([cosine] * 2), jnp.concatenate([sine] * 2))
-    pool = pool.reshape(mp_count, mp_count * PCAP, PAGE, 2 * own_width)
-    pool = lax.all_to_all(pool, "mp", split_axis=0, concat_axis=0, tiled=True)
-    pool = pool.reshape(mp_count, mp_count * PCAP, PAGE, 2, own_width).transpose(1, 2, 3, 0, 4)
-    pool = pool.reshape(mp_count * PCAP, PAGE, 2 * width)
-
+    pool_rows = mp_count * PCAP * PAGE
+    pool = pool.reshape(mp_count, pool_rows, 2 * own_width)
     lengths = lax.dynamic_slice_in_dim(prompt_lengths, 2 * prompt_group, 2)
     head_width = experts * HD
     mixed = pl.pallas_call(
@@ -352,13 +613,37 @@
     partial_value = lax.dot_general(
         mixed, outward, (((1,), (1,)), ((), ())), preferred_element_type=jnp.float32
     ).astype(jnp.bfloat16)
-    attended = lax.psum_scatter(partial_value, "mp", scatter_dimension=0, tiled=True)
-    return (attended, pool)
+    block = (mp_count // 2, tok_rows, model_width)
+    vmem = pl.BlockSpec(memory_space=pltpu.VMEM)
+    anywhere = pl.BlockSpec(memory_space=pl.ANY)
+    attended, pool = pl.pallas_call(
+        functools.partial(return_kernel, mp_count),
+        in_specs=[vmem, anywhere],
+        out_specs=[vmem, anywhere],
+        out_shape=[
+            jax.ShapeDtypeStruct((tok_rows, model_width), jnp.bfloat16),
+            jax.ShapeDtypeStruct((pool_rows, 2 * width), jnp.bfloat16),
+        ],
+        scratch_shapes=[
+            pltpu.VMEM(block, jnp.bfloat16),
+            pltpu.VMEM(block, jnp.bfloat16),
+            pltpu.VMEM(block, jnp.bfloat16),
+            pltpu.SemaphoreType.DMA((2,)),
+            pltpu.SemaphoreType.DMA((2, mp_count // 2)),
+            pltpu.SemaphoreType.DMA((2, mp_count // 2)),
+            pltpu.SemaphoreType.DMA((2, mp_count)),
+            pltpu.SemaphoreType.DMA((2, mp_count)),
+        ],
+        compiler_params=pltpu.CompilerParams(
+            collective_id=1, has_side_effects=True, vmem_limit_bytes=40 * 2**20
+        ),
+    )(partial_value.reshape(mp_count, tok_rows, model_width), pool)
+    return (attended, pool.reshape(mp_count * PCAP, PAGE, 2 * width))
 
 
 def on_device(tokens, norm_gain, router, routes, prompt_lengths, wq_train, *others):
     mp_count = lax.axis_size("mp")
-    split_heads = wq_train.shape[0] == mp_count and wq_train.shape[2] // HD % mp_count == 0
+    split_heads = wq_train.shape[0] == mp_count and lax.axis_size("dp") == 4 and wq_train.shape[2] // HD % mp_count == 0
     program = by_head if split_heads else by_expert
     return program(tokens, norm_gain, router, routes, prompt_lengths, wq_train, *others)
 

time: 422 us -> 385 us (0.912)
  Pallas kernels: 17.5 us -> 334 us
  blocking collectives: 265 us -> 0 us
  waiting for transfers between devices: 41.4 us -> 0 us
  local copies, waits for them, and re-layouts: 37.2 us -> 15.6 us
  between operations: 14.7 us -> 0.77 us
  other arithmetic: 11.4 us -> 5.55 us
    pallas_call x0 -> x3, Pallas kernels: none -> 316 us  [the longest x1 214 us: by_head(): pl.pallas_call(functools.partial(exchange_kernel, mp_count), in_specs=[pl...]
    all_to_all x3 -> x0, blocking collectives: 234 us -> none  [the longest x1 104 us: by_head(): lax.all_to_all(inward, 'mp', split_axis=0, concat_axis=0, tiled=True)]
    reduce_scatter x1 -> x0, waiting for transfers between devices: 41.3 us -> none  [by_head(): lax.psum_scatter(partial_value, 'mp', scatter_dimension=0, tiled=True)]
    reshape x11 -> x0, local copies, waits for them, and re-layouts: 31.4 us -> none  [the longest x4 15.1 us: by_owner(): weights.astype(jnp.bfloat16)]
    all_gather x1 -> x0, blocking collectives: 23.4 us -> none  [by_head(): side = lax.all_gather(side, 'mp', axis=0, tiled=True)]
    unnamed x1 -> x0, blocking collectives: 7.32 us -> none
    unnamed x24 -> x26, local copies, waits for them, and re-layouts: 5.66 us -> 12.6 us
    convert_element_type x3 -> x0, other arithmetic: 6.28 us -> none  [the longest x2 5 us: by_owner(): weights.astype(jnp.bfloat16)]
  transfers between devices with their start and end apart: 4 -> 0, of which waited for: 1 -> 0; matrix products, arithmetic and copies ran while one was open for 14% -> 0% of each run, Pallas kernels for 4% -> 0%
where the time goes in v2:
time: 385 us
  Pallas kernels  334 us (87%)
  matrix products  29 us (8%)
  local copies, waits for them, and re-layouts  15.6 us (4%)
  other arithmetic  5.55 us (1%)
    pallas_call x1, Pallas kernels, by_head(): pl.pallas_call(functools.partial(exchange_kernel, mp_count), in_specs=[pl...  214 us
    pallas_call x1, Pallas kernels, by_head(): pl.pallas_call(functools.partial(return_kernel, mp_count), in_specs=[vmem...  101 us
    dot_general x1, matrix products, by_head(): projected = jnp.dot(segment, inward, preferred_element_type=jnp.float32)  17.3 us
    pallas_call x1, Pallas kernels, by_head(): pl.pallas_call(functools.partial(attention_kernel, experts), grid=(2, hea...  14.3 us
    unnamed x26, local copies, waits for them, and re-layouts  12.6 us
    dot_general x1, matrix products, by_head(): lax.dot_general(mixed, outward, (((1,), (1,)), ((), ())), preferred_eleme...  11.5 us

profile of v2, /device:TPU:9, one launch (start us, length us, event | category | flops | bytes accessed | tf_op | source)
XLA Modules:
  0.0 385.0 jit_solution(6673064698390584085)
XLA Ops:
  0.6 0.0 copy-start
  0.6 1.2 fusion
  1.9 1.2 fusion.2.normed_ref
  3.1 0.8 slice_bitcast_fusion
  3.9 0.2 select_reduce_fusion.2
  4.2 0.7 convert_element_type.16
  4.9 0.1 copy.15
  5.0 0.6 pad.8.side_ref
  5.6 1.2 copy-done.2
  6.9 2.2 copy-done.3
  9.1 2.2 copy-done.4
  11.2 1.6 shard_map.104
  12.9 1.5 copy-done.5
  14.4 1.3 copy-done.6
  15.7 0.6 pad.9.table_ref
  16.3 214.3 %shard_map.105 = (bf16[32,64,2560]{2,1,0:T(8,128)(2,1)}, bf16[32,64,2048]{2,1,0:T(8,128)(2,1)}, bf16[8,128,2048]{2,1,0:T(8,128)(2,1)}, f32[8,128,128]{2,1,0:T(8,128)}, s32[8,8,128]{2,1,0:T(8,128)}) custom-call(bf16[8,64,2560]{2,1,0:T(8,128)(2,1)} %copy-done.5, bf16[8,64,2048]{2,1,0:T(8,128)(2,1)} %copy-done.6, bf16[128,2048]{1,0:T(8,128)(2,1)} %copy-done.9, ...), custom_call_target="tpu_custom_call" | custom-call | tf_op jit(solution)/shard_map/pallas_call | solution.py:536
  230.6 17.3 %fusion.6.raw_ref = f32[1024,2560]{1,0:T(8,128)} fusion(bf16[1024,2048]{1,0:T(8,128)(2,1)} %bitcast.29, bf16[2048,2560]{1,0:T(8,128)(2,1)} %bitcast.27), kind=kOutput, calls=%fused_computation.30 | convolution fusion | flops 10737418240 | bytes 25165824 | tf_op jit(solution)/shard_map/dot_general | solution.py:562
  247.9 0.8 slice_reduce_fusion
  248.7 0.1 eq.53
  248.8 0.1 select_reduce_fusion
  248.9 1.0 fusion.5
  249.9 0.3 maximum_maximum_fusion
  250.2 3.2 shard_map.106
  253.5 0.9 pad_maximum_fusion
  254.4 0.1 dynamic_slice.3.length_ref
  254.5 0.9 copy-done.7
  255.4 1.0 copy-done.8
  256.5 14.3 %shard_map.107 = bf16[1024,2048]{1,0:T(8,128)(2,1)S(1)} custom-call(s32[2]{0:T(128)S(1)} %dynamic_slice.3.length_ref, f32[1024,2560]{1,0:T(8,128)} %fusion.6.raw_ref, bf16[1024,512]{1,0:T(8,128)(2,1)S(1)} %get-tuple-element.18.key_ref.value_ref, bf16[1024,512]{1,0:T(8,128)(2,1)S(1)} %get-tuple-element.18.key_ref.value_ref, ...), custom_call_target="tpu_custom_call" | custom-call | tf_op jit(solution)/shard_map/pallas_call | solution.py:597
  270.8 11.5 %convolution_convert_fusion = bf16[1024,2048]{1,0:T(8,128)(2,1)S(1)} fusion(bf16[1024,2048]{1,0:T(8,128)(2,1)S(1)} %shard_map.107, bf16[2048,2048]{1,0:T(8,128)(2,1)} %bitcast.28), kind=kOutput, calls=%fused_computation | convolution fusion | flops 8592031744 | bytes 16777216 | tf_op jit(solution)/shard_map/dot_general | solution.py:613
  282.3 100.6 %shard_map.108 = (bf16[128,2048]{1,0:T(8,128)(2,1)S(1)}, bf16[256,4096]{1,0:T(8,128)(2,1)S(1)}) custom-call(bf16[8,128,2048]{2,1,0:T(8,128)(2,1)S(1)} %bitcast.22, bf16[8,256,512]{2,1,0:T(8,128)(2,1)S(1)} %bitcast.23), custom_call_target="tpu_custom_call" | custom-call | tf_op jit(solution)/shard_map/pallas_call | solution.py:619
  382.9 0.8 copy.18
  383.7 1.3 copy.19
  (22 shorter events, 0.1 us)
Async XLA Ops:
  0.6 3.3 copy-start
  3.1 9.7 %copy-start.9 = (bf16[128,2048]{1,0:T(8,128)(2,1)}, bf16[128,2048]{1,0:T(8,128)(2,1)S(1)}, u32[]{:S(2)}) copy-start(bf16[128,2048]{1,0:T(8,128)(2,1)S(1)} %fusion.2.normed_ref) | copy-start | bytes 1572868
  5.6 1.2 copy-start.2
  6.9 2.2 copy-start.3
  9.1 2.2 copy-start.4
  11.2 4.5 %copy-start.10 = (s32[1,1,8]{2,1,0:T(1,128)S(1)}, s32[1,1,8]{2,1,0:T(1,128)}, u32[]{:S(2)}) copy-start(s32[1,1,8]{2,1,0:T(1,128)} %param.17) | copy-start | bytes 100
  12.8 1.5 copy-start.5
  14.4 1.3 copy-start.6
  250.2 4.2 %copy-start.11 = (s32[8]{0:T(128)S(1)}, s32[8]{0:T(128)}, u32[]{:S(2)}) copy-start(s32[8]{0:T(128)} %param.13) | copy-start | bytes 100
  254.5 1.0 copy-start.7
  255.4 1.0 copy-start.8
  282.2 102.7 %copy-start.1 = (bf16[2048,8]{0,1:T(8,128)(2,1)S(1)}, bf16[2048,8]{0,1:T(8,128)(2,1)}, u32[]{:S(2)}) copy-start(bf16[2048,8]{0,1:T(8,128)(2,1)} %param.11) | copy-start | bytes 98308

commit v3 on v2

--- a/solution.py
+++ b/solution.py
@@ -10,6 +10,8 @@
 HD = 128
 PAGE = 16
 PCAP = 2
+WINDOW = 3
+LATE = 4
 
 
 def rotate(vectors, positions):
@@ -203,7 +205,7 @@
 
     def place(cell, carry):
         page = source_ref[cell]
-        start = pl.multiple_of(jnp.maximum(page, 0) * PAGE, PAGE)
+        start = pl.multiple_of(jnp.clip(page, 0, kv_ref.shape[0] // PAGE - 1) * PAGE, PAGE)
         content = kv_ref[pl.ds(start, PAGE), :]
         pool_ref[pl.ds(pl.multiple_of(cell * PAGE, PAGE), PAGE), :] = jnp.where(
             page >= 0, content, jnp.zeros_like(content)
@@ -285,6 +287,10 @@
     recv_sem,
     send_small,
     recv_small,
+    chain_send,
+    chain_recv,
+    aside_send,
+    aside_recv,
 ):
     d = lax.axis_index("dp")
     m = lax.axis_index("mp")
@@ -333,17 +339,110 @@
         pltpu.make_async_copy(side_ref, side_all.at[m], local_sem.at[3]),
         pltpu.make_async_copy(table_ref, table_all.at[m], local_sem.at[4]),
     ]
-    for part in range(2):
-        for k in range(1, mp_count):
+    pending = [
+        (part, k) for part in range(2) for k in range(1, mp_count)
+    ]
+
+    def launch(count):
+        for part, k in pending[:count]:
             to = shifted(k)
             send(parts[part].at[to], wholes[part].at[own], wide, (part, 0, k), (d, to))
-        if part == 0:
-            for k in range(1, lines):
-                send(normed_ref, normed_all.at[m], small, (2, k), (d, shifted(2 * k)))
-            for k in range(1, mp_count):
-                to = shifted(k)
-                send(side_ref, side_all.at[m], small, (0, k), (d, to))
-                send(table_ref, table_all.at[m], small, (1, k), (d, to))
+        del pending[:count]
+
+    line = m // 2
+    far_end = lines - 1
+
+    def origin(way, k):
+        return shifted(-2 * k) if way == 0 else shifted(2 * k)
+
+    def has(way, k):
+        return line >= k if way == 0 else line + k <= far_end
+
+    def goes_on(way):
+        return line < far_end if way == 0 else line > 0
+
+    def hop(way, k, block):
+        row = origin(way, k)
+        return pltpu.make_async_remote_copy(
+            src_ref=block,
+            dst_ref=normed_all.at[row],
+            send_sem=chain_send.at[way, k],
+            recv_sem=chain_recv.at[way, k],
+            device_id=(d, shifted(2) if way == 0 else shifted(-2)),
+            device_id_type=pl.DeviceIdType.MESH,
+        )
+
+    def aside(way, k):
+        row = origin(way, k)
+        return pltpu.make_async_remote_copy(
+            src_ref=normed_all.at[row],
+            dst_ref=normed_all.at[row],
+            send_sem=aside_send.at[way, k],
+            recv_sem=aside_recv.at[way, k],
+            device_id=(d, beside),
+            device_id_type=pl.DeviceIdType.MESH,
+        )
+
+    def chain(way, k, block):
+        if k == 0:
+
+            @pl.when(goes_on(way))
+            def _():
+                hop(way, 0, block).start()
+
+            return
+
+        @pl.when(has(way, k))
+        def _():
+            row = origin(way, k)
+            pltpu.make_async_remote_copy(
+                src_ref=normed_all.at[row],
+                dst_ref=normed_all.at[row],
+                send_sem=chain_send.at[way, k - 1],
+                recv_sem=chain_recv.at[way, k - 1],
+                device_id=(d, beside),
+                device_id_type=pl.DeviceIdType.MESH,
+            ).wait_recv()
+            if k < far_end:
+
+                @pl.when(goes_on(way))
+                def _():
+                    hop(way, k, normed_all.at[row]).start()
+
+            aside(way, k).start()
+
+    def chain_end(way, k):
+        if k == 0:
+
+            @pl.when(goes_on(way))
+            def _():
+                hop(way, 0, normed_ref).wait_send()
+
+            return
+
+        @pl.when(has(way, k))
+        def _():
+            row = lax.rem(beside + (-2 * k if way == 0 else 2 * k) + mp_count, mp_count)
+            pltpu.make_async_remote_copy(
+                src_ref=normed_all.at[row],
+                dst_ref=normed_all.at[row],
+                send_sem=aside_send.at[way, k],
+                recv_sem=aside_recv.at[way, k],
+                device_id=(d, beside),
+                device_id_type=pl.DeviceIdType.MESH,
+            ).wait_recv()
+            aside(way, k).wait_send()
+            if k < far_end:
+
+                @pl.when(goes_on(way))
+                def _():
+                    hop(way, k, normed_all.at[origin(way, k)]).wait_send()
+
+    launch(WINDOW)
+    for k in range(1, mp_count):
+        to = shifted(k)
+        send(side_ref, side_all.at[m], small, (0, k), (d, to))
+        send(table_ref, table_all.at[m], small, (1, k), (d, to))
     for copy in locals_:
         copy.start()
 
@@ -359,25 +458,28 @@
         if k > 0:
             arrived(wholes[part].at[slot], wide, (part, 0, k))
             source = wholes[part].at[slot]
+            launch(1)
         send(source, wholes[part].at[slot], wide, (part, 1, k), (across, m))
         send(source, wholes[part].at[slot], wide, (part, 2, k), (twin, m))
         if i >= 2:
             relay(*steps[i - 2])
-        if part == 0 and k < lines:
-            row = shifted(-2 * k)
-            block = normed_ref
-            if k > 0:
-                arrived(normed_all.at[row], small, (2, k))
-                block = normed_all.at[row]
-            send(block, normed_all.at[row], small, (3, k), (d, beside))
+        if (part, k) == (1, LATE):
+            for way in range(2):
+                chain(way, 0, normed_ref)
+            send(normed_ref, normed_all.at[m], small, (3, 0), (d, beside))
     relay(*steps[-2])
     relay(*steps[-1])
+    for k in range(1, lines):
+        for way in range(2):
+            chain(way, k, None)
     for part, k in steps:
         arrived(wholes[part].at[twin * mp_count + shifted(-k)], wide, (part, 2, k))
         far = lax.rem(twin + 2, 4)
         arrived(wholes[part].at[far * mp_count + shifted(-k)], wide, (part, 3, k))
+    arrived(normed_all.at[beside], small, (3, 0))
     for k in range(lines):
-        arrived(normed_all.at[lax.rem(beside - 2 * k + mp_count, mp_count)], small, (3, k))
+        for way in range(2):
+            chain_end(way, k)
     for k in range(1, mp_count):
         arrived(side_all.at[shifted(-k)], small, (0, k))
         arrived(table_all.at[shifted(-k)], small, (1, k))
@@ -550,6 +652,7 @@
             pltpu.SemaphoreType.DMA((2, 4, mp_count)),
             pltpu.SemaphoreType.DMA((4, mp_count)),
             pltpu.SemaphoreType.DMA((4, mp_count)),
+            *[pltpu.SemaphoreType.DMA((2, mp_count // 2))] * 4,
         ],
         compiler_params=pltpu.CompilerParams(collective_id=0, has_side_effects=True),
     )(inward, outward, normed, side, table)

time: 385 us -> 344 us (0.89)
  Pallas kernels: 334 us -> 293 us
    pallas_call x1, Pallas kernels: 214 us -> 172 us  [by_head(): pl.pallas_call(functools.partial(exchange_kernel, mp_count), in_specs=[pl...]
where the time goes in v3:
time: 344 us
  Pallas kernels  293 us (85%)
  matrix products  29 us (8%)
  local copies, waits for them, and re-layouts  15.6 us (5%)
  other arithmetic  5.55 us (2%)
    pallas_call x1, Pallas kernels, by_head(): pl.pallas_call(functools.partial(exchange_kernel, mp_count), in_specs=[pl...  172 us
    pallas_call x1, Pallas kernels, by_head(): pl.pallas_call(functools.partial(return_kernel, mp_count), in_specs=[vmem...  102 us
    dot_general x1, matrix products, by_head(): projected = jnp.dot(segment, inward, preferred_element_type=jnp.float32)  17.3 us
    pallas_call x1, Pallas kernels, by_head(): pl.pallas_call(functools.partial(attention_kernel, experts), grid=(2, hea...  14.3 us
    unnamed x26, local copies, waits for them, and re-layouts  12.6 us
    dot_general x1, matrix products, by_head(): lax.dot_general(mixed, outward, (((1,), (1,)), ((), ())), preferred_eleme...  11.5 us

profile of v3, /device:TPU:9, one launch (start us, length us, event | category | flops | bytes accessed | tf_op | source)
XLA Modules:
  0.0 343.7 jit_solution(2494141897776730824)
XLA Ops:
  0.6 0.0 copy-start
  0.6 1.2 fusion
  1.9 1.2 fusion.2.normed_ref
  3.1 0.8 slice_bitcast_fusion
  3.9 0.2 select_reduce_fusion.2
  4.2 0.7 convert_element_type.16
  4.9 0.1 copy.15
  5.0 0.6 pad.8.side_ref
  5.6 1.2 copy-done.2
  6.9 2.2 copy-done.3
  9.1 2.2 copy-done.4
  11.2 1.6 shard_map.104
  12.9 1.5 copy-done.5
  14.4 1.3 copy-done.6
  15.7 0.6 pad.9.table_ref
  16.3 171.6 %shard_map.105 = (bf16[32,64,2560]{2,1,0:T(8,128)(2,1)}, bf16[32,64,2048]{2,1,0:T(8,128)(2,1)}, bf16[8,128,2048]{2,1,0:T(8,128)(2,1)}, f32[8,128,128]{2,1,0:T(8,128)}, s32[8,8,128]{2,1,0:T(8,128)}) custom-call(bf16[8,64,2560]{2,1,0:T(8,128)(2,1)} %copy-done.5, bf16[8,64,2048]{2,1,0:T(8,128)(2,1)} %copy-done.6, bf16[128,2048]{1,0:T(8,128)(2,1)} %copy-done.9, ...), custom_call_target="tpu_custom_call" | custom-call | tf_op jit(solution)/shard_map/pallas_call | solution.py:638
  187.9 17.3 %fusion.6.raw_ref = f32[1024,2560]{1,0:T(8,128)} fusion(bf16[1024,2048]{1,0:T(8,128)(2,1)} %bitcast.29, bf16[2048,2560]{1,0:T(8,128)(2,1)} %bitcast.27), kind=kOutput, calls=%fused_computation.30 | convolution fusion | flops 10737418240 | bytes 25165824 | tf_op jit(solution)/shard_map/dot_general | solution.py:665
  205.3 0.8 slice_reduce_fusion
  206.0 0.1 eq.53
  206.1 0.1 select_reduce_fusion
  206.2 1.0 fusion.5
  207.2 0.3 maximum_maximum_fusion
  207.6 3.3 shard_map.106
  210.9 0.9 pad_maximum_fusion
  211.8 0.1 dynamic_slice.3.length_ref
  211.9 0.9 copy-done.7
  212.8 1.0 copy-done.8
  213.9 14.3 %shard_map.107 = bf16[1024,2048]{1,0:T(8,128)(2,1)S(1)} custom-call(s32[2]{0:T(128)S(1)} %dynamic_slice.3.length_ref, f32[1024,2560]{1,0:T(8,128)} %fusion.6.raw_ref, bf16[1024,512]{1,0:T(8,128)(2,1)S(1)} %get-tuple-element.18.key_ref.value_ref, bf16[1024,512]{1,0:T(8,128)(2,1)S(1)} %get-tuple-element.18.key_ref.value_ref, ...), custom_call_target="tpu_custom_call" | custom-call | tf_op jit(solution)/shard_map/pallas_call | solution.py:700
  228.2 11.5 %convolution_convert_fusion = bf16[1024,2048]{1,0:T(8,128)(2,1)S(1)} fusion(bf16[1024,2048]{1,0:T(8,128)(2,1)S(1)} %shard_map.107, bf16[2048,2048]{1,0:T(8,128)(2,1)} %bitcast.28), kind=kOutput, calls=%fused_computation | convolution fusion | flops 8592031744 | bytes 16777216 | tf_op jit(solution)/shard_map/dot_general | solution.py:716
  239.7 101.9 %shard_map.108 = (bf16[128,2048]{1,0:T(8,128)(2,1)S(1)}, bf16[256,4096]{1,0:T(8,128)(2,1)S(1)}) custom-call(bf16[8,128,2048]{2,1,0:T(8,128)(2,1)S(1)} %bitcast.22, bf16[8,256,512]{2,1,0:T(8,128)(2,1)S(1)} %bitcast.23), custom_call_target="tpu_custom_call" | custom-call | tf_op jit(solution)/shard_map/pallas_call | solution.py:722
  341.5 0.8 copy.18
  342.3 1.3 copy.19
  (22 shorter events, 0.1 us)
Async XLA Ops:
  0.6 3.3 copy-start
  3.1 9.7 %copy-start.9 = (bf16[128,2048]{1,0:T(8,128)(2,1)}, bf16[128,2048]{1,0:T(8,128)(2,1)S(1)}, u32[]{:S(2)}) copy-start(bf16[128,2048]{1,0:T(8,128)(2,1)S(1)} %fusion.2.normed_ref) | copy-start | bytes 1572868
  5.6 1.2 copy-start.2
  6.9 2.2 copy-start.3
  9.1 2.2 copy-start.4
  11.2 4.5 %copy-start.10 = (s32[1,1,8]{2,1,0:T(1,128)S(1)}, s32[1,1,8]{2,1,0:T(1,128)}, u32[]{:S(2)}) copy-start(s32[1,1,8]{2,1,0:T(1,128)} %param.17) | copy-start | bytes 100
  12.8 1.5 copy-start.5
  14.4 1.3 copy-start.6
  207.6 4.2 %copy-start.11 = (s32[8]{0:T(128)S(1)}, s32[8]{0:T(128)}, u32[]{:S(2)}) copy-start(s32[8]{0:T(128)} %param.13) | copy-start | bytes 100
  211.9 1.0 copy-start.7
  212.8 1.0 copy-start.8
  239.7 104.0 %copy-start.1 = (bf16[2048,8]{0,1:T(8,128)(2,1)S(1)}, bf16[2048,8]{0,1:T(8,128)(2,1)}, u32[]{:S(2)}) copy-start(bf16[2048,8]{0,1:T(8,128)(2,1)} %param.11) | copy-start | bytes 98308
